TPU v7x, 32 devices: a whole 2x2x4 slice. The times are simulated.
32 devices in a mesh: blk: 8 (over z, x), inner: 4 (over y, core).
Axes of the slice: x: 2, y: 2, z: 4, core: 2. Of those that a mesh axis runs over, the one named last changes fastest.
Arguments:
- tokens: bfloat16 [4096, 4096], P(('blk', 'inner')), may hold values from -6 to 6
- expert_ids: int32 [4096, 8], P(('blk', 'inner')), may hold values from 0 to 15, all different within a row; in each aligned block of 128 rows (0 to 127, 128 to 255, ...) at most 96 rows name the same one
- route_weights: float32 [4096, 8], P(('blk', 'inner')), may hold values from 0.1 to 1
- w_in: bfloat16 [32, 4096, 768], P(('blk', 'inner')), may hold values from -0.09375 to 0.09375
- w_out: bfloat16 [32, 384, 4096], P(('blk', 'inner')), may hold values from -0.3125 to 0.3125
Outputs:
- moe_out: bfloat16 [4096, 4096], P(('blk', 'inner'))
Inputs may be any that keep to these rules, and one draw needn't show every extreme that they name: `expert_ids`: each row names 8 different experts; among the 128 rows of one device no expert is named more than 96 times, a bound that some block reaches.
All inputs are finite; a program needn't handle non-finite values.
Results may differ from a plain program's by a relative error of at most 0.0085.
Values may be sent and summed in bfloat16 or wider, within the bound.
A program may use at most 128 MiB of HBM per device.

v0:
```python
import jax
import jax.numpy as jnp
from jax import lax
from jax.sharding import PartitionSpec as P

TOPK = 8
SPLIT = 2
STEPS = 3


def passed_along(value, axis, steps):
    count = lax.axis_size(axis)
    pairs = [(source, (source + steps) % count) for source in range(count)]
    return lax.ppermute(value, axis, pairs)


def expert_rows(arrived, w_in_now, w_out_now):
    hidden = w_out_now.shape[1]
    projected = jnp.einsum("jcd,de->jce", arrived, w_in_now[0], preferred_element_type=jnp.float32)
    activated = (jax.nn.silu(projected[..., :hidden]) * projected[..., hidden:]).astype(
        jnp.bfloat16
    )
    return jnp.einsum(
        "jce,ed->jcd", activated, w_out_now[0], preferred_element_type=jnp.float32
    ).astype(jnp.bfloat16)


def dispatch(tokens, expert_ids, route_weights, home_group, group_count, capacity):
    firsts = home_group * group_count + jnp.arange(group_count, dtype=jnp.int32)
    matches = expert_ids[:, :, None] == firsts[None, None, :]
    chosen = jnp.any(matches, axis=1).astype(jnp.int32)
    weighting = jnp.sum(jnp.where(matches, route_weights[:, :, None], 0.0), axis=1)
    position = jnp.cumsum(chosen, axis=0) - chosen
    slot_ids = jnp.arange(capacity, dtype=jnp.int32)
    one_hot = (
        (chosen.T[:, None, :] == 1) & (position.T[:, None, :] == slot_ids[None, :, None])
    ).astype(jnp.bfloat16)
    picked = jnp.einsum("qct,td->qcd", one_hot, tokens, preferred_element_type=jnp.float32).astype(
        jnp.bfloat16
    )
    outgoing = jnp.repeat(picked, SPLIT, axis=0)
    return (one_hot, weighting, outgoing)


def combine(one_hot, weighting, partials):
    group_count, capacity, tok_rows = one_hot.shape
    paired = partials.reshape(group_count, SPLIT, capacity, partials.shape[-1])
    gathered = jnp.einsum("qct,qkcd->qtd", one_hot, paired, preferred_element_type=jnp.float32)
    return jnp.sum(weighting.T[:, :, None] * gathered, axis=0)


def on_device(tokens, expert_ids, route_weights, w_in, w_out):
    inner_count = lax.axis_size("inner")
    blk_count = lax.axis_size("blk")
    group_index = lax.axis_index("blk")
    group_count = inner_count // SPLIT
    tok_rows = tokens.shape[0]
    experts_all = group_count * blk_count
    capacity = max(2, 3 * tok_rows * TOPK // (2 * experts_all))
    current = (w_in, w_out)
    result = jnp.zeros(tokens.shape, jnp.float32)
    for rotation in range(STEPS):
        home_group = jnp.mod(group_index - rotation, blk_count)
        one_hot, weighting, outgoing = dispatch(
            tokens, expert_ids, route_weights, home_group, group_count, capacity
        )
        if rotation > 0:
            current = passed_along((current[0], current[1]), "blk", 1)

        def apply_rows(arrived, weights_now=current):
            return expert_rows(arrived, weights_now[0], weights_now[1])

        def run_rows(arrived, apply_now=apply_rows):
            return lax.all_to_all(
                apply_now(arrived), "inner", split_axis=0, concat_axis=0, tiled=True
            )

        partials = run_rows(
            lax.all_to_all(outgoing, "inner", split_axis=0, concat_axis=0, tiled=True)
        )
        result = result + combine(one_hot, weighting, partials)
    return result.astype(jnp.bfloat16)


def solution(mesh):
    return jax.shard_map(
        on_device,
        mesh=mesh,
        in_specs=(
            P(("blk", "inner"), None),
            P(("blk", "inner"), None),
            P(("blk", "inner"), None),
            P(("blk", "inner"), None, None),
            P(("blk", "inner"), None, None),
        ),
        out_specs=P(("blk", "inner"), None),
        check_vma=False,
    )
```

profile of v0, /device:TPU:3, one launch (start us, length us, event | category | flops | bytes accessed | tf_op | source)
XLA Modules:
  0.0 466.7 jit_solution(14749663551878512412)
XLA Ops:
  0.0 1.3 collective-permute-start
  1.3 0.8 compare_reduce_fusion.1
  2.4 0.6 convolution_convert_fusion.3
  3.0 2.1 broadcast_in_dim.30
  5.1 5.6 %all-to-all-start.4 = ((bf16[4,96,4096]{2,1,0:T(8,128)(2,1)}), bf16[4,96,4096]{2,1,0:T(8,128)(2,1)}, u32[]{:S(2)}, u32[]{:S(2)}) async-start(bf16[4,96,4096]{2,1,0:T(8,128)(2,1)} %bitcast.65), calls=%async_computation.4 | async-start | bytes 6291456 | tf_op jit(solution)/shard_map/all_to_all | solution.py:79
  11.6 35.2 %all-to-all-done.4 = bf16[4,96,4096]{2,1,0:T(8,128)(2,1)} async-done(((bf16[4,96,4096]{2,1,0:T(8,128)(2,1)}), bf16[4,96,4096]{2,1,0:T(8,128)(2,1)}, u32[]{:S(2)}, u32[]{:S(2)}) %all-to-all-start.4) | async-done | bytes 3145760 | tf_op jit(solution)/shard_map/all_to_all | solution.py:79
  46.9 2.0 broadcast_in_dim.28
  48.9 5.5 %all-to-all-start = ((bf16[4,96,4096]{2,1,0:T(8,128)(2,1)}), bf16[4,96,4096]{2,1,0:T(8,128)(2,1)}, u32[]{:S(2)}, u32[]{:S(2)}) async-start(bf16[4,96,4096]{2,1,0:T(8,128)(2,1)} %bitcast.64), calls=%async_computation | async-start | bytes 6291456 | tf_op jit(solution)/shard_map/all_to_all | solution.py:79
  54.8 81.9 %collective-permute-done = bf16[1,4096,768]{2,1,0:T(8,128)(2,1)} collective-permute-done((bf16[1,4096,768]{2,1,0:T(8,128)(2,1)}, bf16[1,4096,768]{2,1,0:T(8,128)(2,1)}, u32[]{:S(2)}, u32[]{:S(2)}) %collective-permute-start) | collective-permute-done | bytes 6291488 | tf_op jit(solution)/shard_map/ppermute | solution.py:14
  136.7 2.2 collective-permute-start.2
  139.4 2.1 broadcast_in_dim.29
  141.6 6.5 %all-to-all-start.2 = ((bf16[4,96,4096]{2,1,0:T(8,128)(2,1)}), bf16[4,96,4096]{2,1,0:T(8,128)(2,1)}, u32[]{:S(2)}, u32[]{:S(2)}) async-start(bf16[4,96,4096]{2,1,0:T(8,128)(2,1)} %bitcast.13), calls=%async_computation.2 | async-start | bytes 6291456 | tf_op jit(solution)/shard_map/all_to_all | solution.py:79
  148.4 6.3 %fusion.4 = f32[4,96,768]{2,1,0:T(8,128)S(1)} fusion(bf16[4,96,4096]{2,1,0:T(8,128)(2,1)} %all-to-all-done, bf16[1,4096,768]{2,1,0:T(8,128)(2,1)} %param.8), kind=kOutput, calls=%fused_computation.7 | convolution fusion | flops 2415919104 | bytes 10616832 | tf_op jit(solution)/shard_map/jcd,de->jce/dot_general | solution.py:19
  154.7 5.5 %convolution_convert_fusion.2 = bf16[4,96,4096]{2,1,0:T(8,128)(2,1)} fusion(bf16[1,384,4096]{2,1,0:T(8,128)(2,1)} %param.9, f32[4,96,768]{2,1,0:T(8,128)S(1)} %fusion.4), kind=kOutput, calls=%fused_computation.11 | convolution fusion | flops 1210417152 | bytes 7471104 | tf_op jit(solution)/shard_map/jce,ed->jcd/dot_general | solution.py:23
  160.2 24.0 %all-to-all-done.2 = bf16[4,96,4096]{2,1,0:T(8,128)(2,1)} async-done(((bf16[4,96,4096]{2,1,0:T(8,128)(2,1)}), bf16[4,96,4096]{2,1,0:T(8,128)(2,1)}, u32[]{:S(2)}, u32[]{:S(2)}) %all-to-all-start.2) | async-done | bytes 3145760 | tf_op jit(solution)/shard_map/all_to_all | solution.py:79
  184.2 4.5 all-to-all-start.1
  188.7 153.7 %collective-permute-done.1 = bf16[1,384,4096]{2,1,0:T(8,128)(2,1)} collective-permute-done((bf16[1,384,4096]{2,1,0:T(8,128)(2,1)}, bf16[1,384,4096]{2,1,0:T(8,128)(2,1)}, u32[]{:S(2)}, u32[]{:S(2)}) %collective-permute-start.1) | collective-permute-done | bytes 3145760 | tf_op jit(solution)/shard_map/ppermute | solution.py:14
  343.0 6.3 %fusion.2 = f32[4,96,768]{2,1,0:T(8,128)S(1)} fusion(bf16[4,96,4096]{2,1,0:T(8,128)(2,1)} %all-to-all-done.2, bf16[1,4096,768]{2,1,0:T(8,128)(2,1)} %collective-permute-done), kind=kOutput, calls=%fused_computation.5 | convolution fusion | flops 2415919104 | bytes 10616832 | tf_op jit(solution)/shard_map/jcd,de->jce/dot_general | solution.py:19
  349.3 5.5 %convolution_convert_fusion.1 = bf16[4,96,4096]{2,1,0:T(8,128)(2,1)} fusion(bf16[1,384,4096]{2,1,0:T(8,128)(2,1)} %collective-permute-done.1, f32[4,96,768]{2,1,0:T(8,128)S(1)} %fusion.2), kind=kOutput, calls=%fused_computation.10 | convolution fusion | flops 1210417152 | bytes 7471104 | tf_op jit(solution)/shard_map/jce,ed->jcd/dot_general | solution.py:23
  354.8 7.4 %all-to-all-start.3 = ((bf16[4,96,4096]{2,1,0:T(8,128)(2,1)}), bf16[4,96,4096]{2,1,0:T(8,128)(2,1)}, u32[]{:S(2)}, u32[]{:S(2)}) async-start(bf16[4,96,4096]{2,1,0:T(8,128)(2,1)} %convolution_convert_fusion.1), calls=%async_computation.3 | async-start | bytes 6291456 | tf_op jit(solution)/shard_map/all_to_all | solution.py:74
  362.2 6.3 %fusion = f32[4,96,768]{2,1,0:T(8,128)S(1)} fusion(bf16[4,96,4096]{2,1,0:T(8,128)(2,1)} %all-to-all-done.4, bf16[1,4096,768]{2,1,0:T(8,128)(2,1)} %collective-permute-done.2), kind=kOutput, calls=%fused_computation.3 | convolution fusion | flops 2415919104 | bytes 10616832 | tf_op jit(solution)/shard_map/jcd,de->jce/dot_general | solution.py:19
  368.5 44.3 %collective-permute-done.3 = bf16[1,384,4096]{2,1,0:T(8,128)(2,1)} collective-permute-done((bf16[1,384,4096]{2,1,0:T(8,128)(2,1)}, bf16[1,384,4096]{2,1,0:T(8,128)(2,1)}, u32[]{:S(2)}, u32[]{:S(2)}) %collective-permute-start.3) | collective-permute-done | bytes 3145760 | tf_op jit(solution)/shard_map/ppermute | solution.py:14
  412.8 5.4 %convolution_convert_fusion = bf16[4,96,4096]{2,1,0:T(8,128)(2,1)} fusion(bf16[1,384,4096]{2,1,0:T(8,128)(2,1)} %collective-permute-done.3, f32[4,96,768]{2,1,0:T(8,128)S(1)} %fusion), kind=kOutput, calls=%fused_computation.9 | convolution fusion | flops 1210417152 | bytes 7471104 | tf_op jit(solution)/shard_map/jce,ed->jcd/dot_general | solution.py:23
  418.2 7.5 %all-to-all-start.5 = ((bf16[4,96,4096]{2,1,0:T(8,128)(2,1)}), bf16[4,96,4096]{2,1,0:T(8,128)(2,1)}, u32[]{:S(2)}, u32[]{:S(2)}) async-start(bf16[4,96,4096]{2,1,0:T(8,128)(2,1)} %convolution_convert_fusion), calls=%async_computation.5 | async-start | bytes 6291456 | tf_op jit(solution)/shard_map/all_to_all | solution.py:74
  425.9 0.6 convert_reduce_fusion.2
  426.5 0.8 fusion.9
  427.3 2.5 convert_reduce_fusion.1
  429.8 2.1 fusion.10
  431.9 30.0 %all-to-all-done.5 = bf16[4,96,4096]{2,1,0:T(8,128)(2,1)} async-done(((bf16[4,96,4096]{2,1,0:T(8,128)(2,1)}), bf16[4,96,4096]{2,1,0:T(8,128)(2,1)}, u32[]{:S(2)}, u32[]{:S(2)}) %all-to-all-start.5) | async-done | bytes 3145760 | tf_op jit(solution)/shard_map/all_to_all | solution.py:74
  461.9 2.6 convert_reduce_fusion
  464.6 0.8 fusion.11
  465.4 1.3 add_convert_fusion
  (36 shorter events, 3.2 us)
Async XLA Ops:
  0.0 2.4 copy-start
  0.0 136.7 %collective-permute-start = (bf16[1,4096,768]{2,1,0:T(8,128)(2,1)}, bf16[1,4096,768]{2,1,0:T(8,128)(2,1)}, u32[]{:S(2)}, u32[]{:S(2)}) collective-permute-start(bf16[1,4096,768]{2,1,0:T(8,128)(2,1)} %param.8), channel_id=1, source_target_pairs={{0,4},{4,8},{8,12},{12,16},{16,20},{20,24},{24,28},{28,0},{1,5},{5... | collective-permute-start | bytes 18874376 | tf_op jit(solution)/shard_map/ppermute | solution.py:14
  5.1 41.8 %all-to-all-start.4 = ((bf16[4,96,4096]{2,1,0:T(8,128)(2,1)}), bf16[4,96,4096]{2,1,0:T(8,128)(2,1)}, u32[]{:S(2)}, u32[]{:S(2)}) async-start(bf16[4,96,4096]{2,1,0:T(8,128)(2,1)} %bitcast.65), calls=%async_computation.4 | async-start | bytes 6291456 | tf_op jit(solution)/shard_map/all_to_all | solution.py:79
  48.9 90.5 %all-to-all-start = ((bf16[4,96,4096]{2,1,0:T(8,128)(2,1)}), bf16[4,96,4096]{2,1,0:T(8,128)(2,1)}, u32[]{:S(2)}, u32[]{:S(2)}) async-start(bf16[4,96,4096]{2,1,0:T(8,128)(2,1)} %bitcast.64), calls=%async_computation | async-start | bytes 6291456 | tf_op jit(solution)/shard_map/all_to_all | solution.py:79
  136.7 225.5 %collective-permute-start.2 = (bf16[1,4096,768]{2,1,0:T(8,128)(2,1)}, bf16[1,4096,768]{2,1,0:T(8,128)(2,1)}, u32[]{:S(2)}, u32[]{:S(2)}) collective-permute-start(bf16[1,4096,768]{2,1,0:T(8,128)(2,1)} %collective-permute-done), channel_id=1, source_target_pairs={{0,4},{4,8},{8,12},{12,16},{16,20},{20,24},{24,28},{28,0},{1,5},{5... | collective-permute-start | bytes 18874376 | tf_op jit(solution)/shard_map/ppermute | solution.py:14
  141.6 42.6 %all-to-all-start.2 = ((bf16[4,96,4096]{2,1,0:T(8,128)(2,1)}), bf16[4,96,4096]{2,1,0:T(8,128)(2,1)}, u32[]{:S(2)}, u32[]{:S(2)}) async-start(bf16[4,96,4096]{2,1,0:T(8,128)(2,1)} %bitcast.13), calls=%async_computation.2 | async-start | bytes 6291456 | tf_op jit(solution)/shard_map/all_to_all | solution.py:79
  148.0 194.4 %collective-permute-start.1 = (bf16[1,384,4096]{2,1,0:T(8,128)(2,1)}, bf16[1,384,4096]{2,1,0:T(8,128)(2,1)}, u32[]{:S(2)}, u32[]{:S(2)}) collective-permute-start(bf16[1,384,4096]{2,1,0:T(8,128)(2,1)} %param.9), channel_id=1, source_target_pairs={{0,4},{4,8},{8,12},{12,16},{16,20},{20,24},{24,28},{28,0},{1,5},{5... | collective-permute-start | bytes 9437192 | tf_op jit(solution)/shard_map/ppermute | solution.py:14
  184.2 170.6 %all-to-all-start.1 = ((bf16[4,96,4096]{2,1,0:T(8,128)(2,1)}), bf16[4,96,4096]{2,1,0:T(8,128)(2,1)S(1)}, u32[]{:S(2)}, u32[]{:S(2)}) async-start(bf16[4,96,4096]{2,1,0:T(8,128)(2,1)} %convolution_convert_fusion.2), calls=%async_computation.1 | async-start | bytes 6291456 | tf_op jit(solution)/shard_map/all_to_all | solution.py:74
  342.4 70.4 %collective-permute-start.3 = (bf16[1,384,4096]{2,1,0:T(8,128)(2,1)}, bf16[1,384,4096]{2,1,0:T(8,128)(2,1)}, u32[]{:S(2)}, u32[]{:S(2)}) collective-permute-start(bf16[1,384,4096]{2,1,0:T(8,128)(2,1)} %collective-permute-done.1), channel_id=1, source_target_pairs={{0,4},{4,8},{8,12},{12,16},{16,20},{20,24},{24,28},{28,0},{1,5},{5... | collective-permute-start | bytes 9437192 | tf_op jit(solution)/shard_map/ppermute | solution.py:14
  354.8 63.5 %all-to-all-start.3 = ((bf16[4,96,4096]{2,1,0:T(8,128)(2,1)}), bf16[4,96,4096]{2,1,0:T(8,128)(2,1)}, u32[]{:S(2)}, u32[]{:S(2)}) async-start(bf16[4,96,4096]{2,1,0:T(8,128)(2,1)} %convolution_convert_fusion.1), calls=%async_computation.3 | async-start | bytes 6291456 | tf_op jit(solution)/shard_map/all_to_all | solution.py:74
  418.2 7.5 %copy-start.3 = (s32[128,8]{0,1:T(8,128)S(1)}, s32[128,8]{0,1:T(8,128)}, u32[]{:S(2)}) copy-start(s32[128,8]{0,1:T(8,128)} %param.6) | copy-start | bytes 12292
  418.2 7.5 %copy-start.4 = (f32[128,8]{0,1:T(8,128)S(1)}, f32[128,8]{0,1:T(8,128)}, u32[]{:S(2)}) copy-start(f32[128,8]{0,1:T(8,128)} %param.7) | copy-start | bytes 12292
  418.2 43.7 %all-to-all-start.5 = ((bf16[4,96,4096]{2,1,0:T(8,128)(2,1)}), bf16[4,96,4096]{2,1,0:T(8,128)(2,1)}, u32[]{:S(2)}, u32[]{:S(2)}) async-start(bf16[4,96,4096]{2,1,0:T(8,128)(2,1)} %convolution_convert_fusion), calls=%async_computation.5 | async-start | bytes 6291456 | tf_op jit(solution)/shard_map/all_to_all | solution.py:74
  461.9 3.5 copy-start.2
  464.6 2.1 copy-start.1
where the time goes:
time: 473 us; the launch traced here: 467 us
  waiting for transfers between devices  369 us (78%)
  starting transfers between devices  41.3 us (9%)
  matrix products  40.8 us (9%)
  other arithmetic  8.42 us (2%)
  local copies, waits for them, and re-layouts  6.78 us (1%)
    ppermute x4, waiting for transfers between devices, passed_along(): return lax.ppermute(value, axis, pairs)  280 us
    all_to_all x3, waiting for transfers between devices, on_device(): lax.all_to_all(outgoing, 'inner', split_axis=0, concat_axis=0, tiled=True)  59.2 us
    all_to_all x3, waiting for transfers between devices, run_rows(): lax.all_to_all(apply_now(arrived), 'inner', split_axis=0, concat_axis=0,...  30 us
    all_to_all x3, starting transfers between devices, run_rows(): lax.all_to_all(apply_now(arrived), 'inner', split_axis=0, concat_axis=0,...  19.4 us
    dot_general x3, matrix products, expert_rows(): jnp.einsum('jcd,de->jce', arrived, w_in_now[0], preferred_element_type=jn...  19 us
    all_to_all x3, starting transfers between devices, on_device(): lax.all_to_all(outgoing, 'inner', split_axis=0, concat_axis=0, tiled=True)  17.5 us
    dot_general x3, matrix products, expert_rows(): jnp.einsum('jce,ed->jcd', activated, w_out_now[0], preferred_element_type...  16.4 us
  transfers between devices with their start and end apart: 10, of which 6 were waited for; matrix products, arithmetic and copies ran while one was open for 11% of the time, Pallas kernels for 0%

commit v1 on v0

v1 whole, which is shorter than its diff:
```python
import jax
import jax.numpy as jnp
from jax import lax
from jax.experimental import pallas as pl
from jax.experimental.pallas import tpu as pltpu
from jax.sharding import PartitionSpec as P

SPLIT = 2
STEPS = 3
CHUNKS = 4
MESH = pl.DeviceIdType.MESH


def passed_along(value, axis, steps):
    count = lax.axis_size(axis)
    pairs = [(source, (source + steps) % count) for source in range(count)]
    return lax.ppermute(value, axis, pairs)


def on_device_general(tokens, expert_ids, route_weights, w_in, w_out):
    inner_count = lax.axis_size("inner")
    blk_count = lax.axis_size("blk")
    hidden = w_out.shape[1]
    gathered, ids, scales = (
        lax.all_gather(v, "inner", axis=0, tiled=True) for v in (tokens, expert_ids, route_weights)
    )
    current = (w_in, w_out)
    result = jnp.zeros(gathered.shape, jnp.float32)
    for rotation in range(STEPS):
        home = jnp.mod(lax.axis_index("blk") - rotation, blk_count)
        expert = home * (inner_count // SPLIT) + lax.axis_index("inner") // SPLIT
        if rotation > 0:
            current = passed_along(current, "blk", 1)
        scale = jnp.sum(jnp.where(ids == expert, scales, 0.0), axis=1, keepdims=True)
        projected = jnp.dot(gathered, current[0][0], preferred_element_type=jnp.float32)
        activated = (jax.nn.silu(projected[:, :hidden]) * projected[:, hidden:]).astype(jnp.bfloat16)
        partial = jnp.dot(activated, current[1][0], preferred_element_type=jnp.float32)
        result = result + scale * partial
    return lax.psum_scatter(
        result.astype(jnp.bfloat16), "inner", scatter_dimension=0, tiled=True
    ).astype(jnp.bfloat16)


def moe_kernel(
    tok_ref, aux_ref, w_in_ref, w_out_ref, out_ref,
    x_ref, aux_all, w_in_vm, w_out_vm, proj, act,
    own, sib_out, sib_in, from_x, from_y, from_z,
    local_sem, xs, xr, us, ur, qs, qr, a_s, a_r, b_s, b_r, z_s, z_r,
):
    blk = lax.axis_size("blk")
    h, i = lax.axis_index("blk"), lax.axis_index("inner")
    tok = tok_ref.shape[0]
    rows = tok // CHUNKS
    hidden = w_out_vm.shape[0]
    model = w_out_vm.shape[1]
    x = lax.rem(h, 2)
    y, k = i // 2, lax.rem(i, 2)
    r_of_x = 2 * (1 - x)
    sib = (h, 2 * y + 1 - k)
    y_dev = (h, 2 * (1 - y) + k)
    x_dev = (h + 1 - 2 * x, i)
    z_down = (lax.rem(h + blk - 2, blk), i)
    z_up = (lax.rem(h + 2, blk), i)

    def part(c):
        return pl.ds(c * rows, rows)

    def slot_rows(dk, c):
        return pl.ds(dk * tok + c * rows, rows)

    def remote(src, dst, s, r, device):
        return pltpu.make_async_remote_copy(
            src_ref=src, dst_ref=dst, send_sem=s, recv_sem=r, device_id=device, device_id_type=MESH
        )

    def x_copy(slot, c, src, device):
        r, dy, dk = slot
        at = (r * 2 + dy) * 2 + dk
        return remote(
            src, x_ref.at[r, dy, slot_rows(dk, c), :], xs.at[at, c], xr.at[at, c], device
        )

    def held(r, dy, c):
        return x_ref.at[r, dy, slot_rows(0, c), :]

    def got(slot, c):
        x_copy(slot, c, held(0, 0, c), sib).wait_recv()

    def aux_copy(r, dy, dk):
        at = (r * 2 + dy) * 2 + dk
        y_to = y if dy == 0 else 1 - y
        k_to = k if dk == 0 else 1 - k
        device = (lax.rem(h + blk - r, blk), 2 * y_to + k_to)
        return remote(aux_ref, aux_all.at[r, dy, dk], us.at[at], ur.at[at], device)

    def q_copy(r, dy):
        at = r * 2 + dy
        return remote(sib_out.at[r, dy], sib_in.at[r, dy], qs.at[at], qr.at[at], sib)

    def a_copy(dy, c):
        return remote(
            own.at[1, dy, part(c), :], from_x.at[dy, part(c), :], a_s.at[dy, c], a_r.at[dy, c], x_dev
        )

    def b_copy(half, c):
        return remote(
            own.at[2 * half, 1, part(c), :], from_y.at[half, part(c), :],
            b_s.at[half, c], b_r.at[half, c], y_dev,
        )

    def z_copy(c):
        return remote(own.at[2, 0, part(c), :], from_z.at[part(c), :], z_s.at[c], z_r.at[c], z_up)

    loads = [
        pltpu.make_async_copy(tok_ref, x_ref.at[0, 0, pl.ds(0, tok), :], local_sem.at[0]),
        pltpu.make_async_copy(w_in_ref.at[0], w_in_vm, local_sem.at[1]),
        pltpu.make_async_copy(w_out_ref.at[0], w_out_vm, local_sem.at[2]),
    ]
    for load in loads:
        load.start()

    barrier = pltpu.get_barrier_semaphore()
    peers = 0
    for r in range(-2, 3):
        for dy in range(2):
            for dk in range(2):
                if (r, dy, dk) == (0, 0, 0):
                    continue
                y_to = y if dy == 0 else 1 - y
                k_to = k if dk == 0 else 1 - k
                pl.semaphore_signal(
                    barrier, inc=1,
                    device_id=(lax.rem(h + blk + r, blk), 2 * y_to + k_to), device_id_type=MESH,
                )
                peers += 1
    pl.semaphore_wait(barrier, peers)

    for c in range(CHUNKS):
        mine = tok_ref.at[part(c), :]
        x_copy((2, 0, 0), c, mine, z_down).start()
        x_copy((0, 1, 0), c, mine, y_dev).start()

        @pl.when(x == 1)
        def _():
            x_copy((1, 0, 0), c, mine, x_dev).start()

        x_copy((0, 0, 1), c, mine, sib).start()
    slots = [(r, dy, dk) for r in range(3) for dy in range(2) for dk in range(2)][1:]
    for slot in slots:
        aux_copy(*slot).start()
    aux_all[0, 0, 0] = aux_ref[...]

    expert = 2 * h + y

    def scale_of(r, dy, dk):
        table = aux_all[r, dy, dk]
        line = jnp.sum(
            jnp.where(lax.broadcasted_iota(jnp.int32, table.shape, 0) == expert, table, 0.0),
            axis=0, keepdims=True,
        )
        square = (tok, tok)
        same = lax.broadcasted_iota(jnp.int32, square, 0) == lax.broadcasted_iota(jnp.int32, square, 1)
        return jnp.sum(
            jnp.where(same, jnp.broadcast_to(line, square), 0.0), axis=1, keepdims=True
        )

    def compute(r, dy):
        for dk in range(2):
            if (r, dy, dk) != (0, 0, 0):
                aux_copy(r, dy, dk).wait_recv()
        for c in range(CHUNKS):
            got((r, dy, 1), c)

        def in_step(n, carry):
            cols = pl.ds(pl.multiple_of(n * 256, 256), 256)
            proj[:, cols] = jnp.dot(x_ref[r, dy], w_in_vm[:, cols], preferred_element_type=jnp.float32)
            return carry

        lax.fori_loop(0, 2 * hidden // 256, in_step, 0)
        for dk in range(2):
            line = pl.ds(dk * tok, tok)
            gate = proj[line, pl.ds(0, hidden)]
            up = proj[line, pl.ds(hidden, hidden)]
            act[line, :] = (gate / (1.0 + jnp.exp(-gate)) * up * scale_of(r, dy, dk)).astype(
                jnp.bfloat16
            )

        def out_step(n, carry):
            cols = pl.ds(pl.multiple_of(n * 512, 512), 512)
            value = jnp.dot(act[...], w_out_vm[:, cols], preferred_element_type=jnp.float32)
            own[r, dy, :, cols] = value[:tok].astype(jnp.bfloat16)
            sib_out[r, dy, :, cols] = value[tok:].astype(jnp.bfloat16)
            return carry

        lax.fori_loop(0, model // 512, out_step, 0)
        q_copy(r, dy).start()

    def add_up(r, dy, c, *more):
        total = own[r, dy, part(c), :].astype(jnp.float32)
        total = total + sib_in[r, dy, part(c), :].astype(jnp.float32)
        for term in more:
            total = total + term.astype(jnp.float32)
        return total

    for load in loads:
        load.wait()
    compute(0, 0)
    for c in range(CHUNKS):
        got((2, 0, 0), c)

        @pl.when(x == 0)
        def _():
            x_copy((1, 0, 0), c, held(2, 0, c), x_dev).start()

        x_copy((2, 1, 0), c, held(2, 0, c), y_dev).start()
        x_copy((2, 0, 1), c, held(2, 0, c), sib).start()
        got((0, 1, 0), c)

        @pl.when(x == 1)
        def _():
            x_copy((1, 1, 0), c, held(0, 1, c), x_dev).start()

        x_copy((0, 1, 1), c, held(0, 1, c), sib).start()
    compute(0, 1)
    compute(2, 0)
    for c in range(CHUNKS):
        got((1, 0, 0), c)
        x_copy((1, 0, 1), c, held(1, 0, c), sib).start()
        got((2, 1, 0), c)

        @pl.when(x == 0)
        def _():
            x_copy((1, 1, 0), c, held(2, 1, c), x_dev).start()

        x_copy((2, 1, 1), c, held(2, 1, c), sib).start()
    compute(1, 0)
    compute(2, 1)
    q_copy(1, 0).wait_recv()
    for c in range(CHUNKS):
        own[1, 0, part(c), :] = add_up(1, 0, c).astype(jnp.bfloat16)
        a_copy(0, c).start()
    q_copy(0, 1).wait_recv()
    q_copy(2, 1).wait_recv()
    r_plain = 2 - r_of_x
    for c in range(CHUNKS):
        own[r_plain, 1, part(c), :] = add_up(r_plain, 1, c).astype(jnp.bfloat16)
        b_copy(r_plain // 2, c).start()
    for c in range(CHUNKS):
        got((1, 1, 0), c)
        x_copy((1, 1, 1), c, held(1, 1, c), sib).start()
    compute(1, 1)
    q_copy(1, 1).wait_recv()
    for c in range(CHUNKS):
        own[1, 1, part(c), :] = add_up(1, 1, c).astype(jnp.bfloat16)
        a_copy(1, c).start()
    q_copy(0, 0).wait_recv()
    q_copy(2, 0).wait_recv()
    for c in range(CHUNKS):
        a_copy(0, c).wait_recv()
        own[r_of_x, 0, part(c), :] = add_up(r_of_x, 0, c, from_x[0, part(c), :]).astype(jnp.bfloat16)
        own[r_plain, 0, part(c), :] = add_up(r_plain, 0, c).astype(jnp.bfloat16)
    for c in range(CHUNKS):
        a_copy(1, c).wait_recv()
        own[r_of_x, 1, part(c), :] = add_up(r_of_x, 1, c, from_x[1, part(c), :]).astype(jnp.bfloat16)
        b_copy(r_of_x // 2, c).start()
    for c in range(CHUNKS):
        b_copy(1, c).wait_recv()
        own[2, 0, part(c), :] = (
            own[2, 0, part(c), :].astype(jnp.float32) + from_y[1, part(c), :].astype(jnp.float32)
        ).astype(jnp.bfloat16)
        z_copy(c).start()
    for c in range(CHUNKS):
        b_copy(0, c).wait_recv()
        z_copy(c).wait_recv()
        out_ref[part(c), :] = (
            own[0, 0, part(c), :].astype(jnp.float32)
            + from_y[0, part(c), :].astype(jnp.float32)
            + from_z[part(c), :].astype(jnp.float32)
        ).astype(jnp.bfloat16)

    for slot in slots:
        aux_copy(*slot).wait_send()
        for c in range(CHUNKS):
            x_copy(slot, c, held(0, 0, c), sib).wait_send()
    for r in range(3):
        for dy in range(2):
            q_copy(r, dy).wait_send()
    for c in range(CHUNKS):
        for half in range(2):
            a_copy(half, c).wait_send()
            b_copy(half, c).wait_send()
        z_copy(c).wait_send()


def on_device_kernel(tokens, expert_ids, route_weights, w_in, w_out):
    tok, model = tokens.shape
    hidden = w_out.shape[1]
    experts = lax.axis_size("inner") // SPLIT * lax.axis_size("blk")
    matches = expert_ids.T[None, :, :] == jnp.arange(experts, dtype=jnp.int32)[:, None, None]
    table = jnp.sum(jnp.where(matches, route_weights.T[None, :, :], 0.0), axis=1)
    hbm = pl.BlockSpec(memory_space=pl.ANY)
    vmem = pl.BlockSpec(memory_space=pltpu.VMEM)
    dma = pltpu.SemaphoreType.DMA
    bf16 = jnp.bfloat16
    return pl.pallas_call(
        moe_kernel,
        out_shape=jax.ShapeDtypeStruct((tok, model), bf16),
        in_specs=[hbm, vmem, hbm, hbm],
        out_specs=vmem,
        scratch_shapes=[
            pltpu.VMEM((3, 2, 2 * tok, model), bf16),
            pltpu.VMEM((3, 2, 2, experts, tok), jnp.float32),
            pltpu.VMEM(w_in.shape[1:], bf16),
            pltpu.VMEM(w_out.shape[1:], bf16),
            pltpu.VMEM((2 * tok, 2 * hidden), jnp.float32),
            pltpu.VMEM((2 * tok, hidden), bf16),
            pltpu.VMEM((3, 2, tok, model), bf16),
            pltpu.VMEM((3, 2, tok, model), bf16),
            pltpu.VMEM((3, 2, tok, model), bf16),
            pltpu.VMEM((2, tok, model), bf16),
            pltpu.VMEM((2, tok, model), bf16),
            pltpu.VMEM((tok, model), bf16),
            dma((3,)),
            dma((12, CHUNKS)),
            dma((12, CHUNKS)),
            dma((12,)),
            dma((12,)),
            dma((6,)),
            dma((6,)),
            dma((2, CHUNKS)),
            dma((2, CHUNKS)),
            dma((2, CHUNKS)),
            dma((2, CHUNKS)),
            dma((CHUNKS,)),
            dma((CHUNKS,)),
        ],
        compiler_params=pltpu.CompilerParams(
            collective_id=0, has_side_effects=True, vmem_limit_bytes=58 * 1024 * 1024
        ),
    )(tokens, table, w_in, w_out)


def solution(mesh):
    small = mesh.shape["inner"] == 4 and mesh.shape["blk"] % 2 == 0 and mesh.shape["blk"] >= 6
    on_device = on_device_kernel if small else on_device_general
    return jax.shard_map(
        on_device,
        mesh=mesh,
        in_specs=(
            P(("blk", "inner"), None),
            P(("blk", "inner"), None),
            P(("blk", "inner"), None),
            P(("blk", "inner"), None, None),
            P(("blk", "inner"), None, None),
        ),
        out_specs=P(("blk", "inner"), None),
        check_vma=False,
    )
```

time: 473 us -> 144 us (0.30); the launches traced: 467 us -> 144 us
  waiting for transfers between devices: 369 us -> 0 us
  Pallas kernels: 0 us -> 140 us
  starting transfers between devices: 41.3 us -> 0 us
  matrix products: 40.8 us -> 0 us
  other arithmetic: 8.42 us -> 1.32 us
    ppermute x4 -> x0, waiting for transfers between devices: 280 us -> none  [passed_along(): return lax.ppermute(value, axis, pairs)]
    pallas_call x0 -> x1, Pallas kernels: none -> 140 us  [on_device_kernel(): pl.pallas_call(moe_kernel, out_shape=jax.ShapeDtypeStruct((tok, model), b...]
    all_to_all x6 -> x0, waiting for transfers between devices: 89.3 us -> none  [the longest x3 59.2 us: on_device(): lax.all_to_all(outgoing, 'inner', split_axis=0, concat_axis=0, tiled=True)]
    dot_general x12 -> x0, matrix products: 40.8 us -> none  [the longest x3 19 us: expert_rows(): jnp.einsum('jcd,de->jce', arrived, w_in_now[0], preferred_element_type=jn...]
    all_to_all x6 -> x0, starting transfers between devices: 37 us -> none  [the longest x3 19.4 us: run_rows(): lax.all_to_all(apply_now(arrived), 'inner', split_axis=0, concat_axis=0,...]
    broadcast_in_dim x3 -> x0, local copies, waits for them, and re-layouts: 6.24 us -> none  [dispatch(): outgoing = jnp.repeat(picked, SPLIT, axis=0)]
  transfers between devices with their start and end apart: 10 -> 0, of which waited for: 6 -> 0; matrix products, arithmetic and copies ran while one was open for 11% -> 0% of each run, Pallas kernels for 0% -> 0%
where the time goes in v1:
time: 144 us
  Pallas kernels  140 us (97%)
  local copies, waits for them, and re-layouts  2.29 us (2%)
    pallas_call x1, Pallas kernels, on_device_kernel(): pl.pallas_call(moe_kernel, out_shape=jax.ShapeDtypeStruct((tok, model), b...  140 us

profile of v1, /device:TPU:3, one launch (start us, length us, event | category | flops | bytes accessed | tf_op | source)
XLA Modules:
  0.0 144.0 jit_solution(11555093613406086393)
XLA Ops:
  0.0 1.3 select_reduce_fusion.aux_ref
  1.3 140.3 %shard_map.55 = bf16[128,4096]{1,0:T(8,128)(2,1)} custom-call(bf16[128,4096]{1,0:T(8,128)(2,1)} %tok_ref.1, f32[16,128]{1,0:T(8,128)} %select_reduce_fusion.aux_ref, bf16[1,4096,768]{2,1,0:T(8,128)(2,1)} %w_in_ref.1, bf16[1,384,4096]{2,1,0:T(8,128)(2,1)} %w_out_ref.1), custom_call_target="tpu_custom_call" | custom-call | tf_op jit(solution)/shard_map/pallas_call | solution.py:305
  141.7 2.3 %copy.7 = bf16[128,4096]{1,0:T(8,128)(2,1)} copy(bf16[128,4096]{1,0:T(8,128)(2,1)} %shard_map.55) | data formatting | bytes 2097152

commit v2 on v1

--- a/solution.py
+++ b/solution.py
@@ -8,6 +8,8 @@
 SPLIT = 2
 STEPS = 3
 CHUNKS = 4
+EARLY = (0, 1)
+LATE = (2, 3)
 MESH = pl.DeviceIdType.MESH
 
 
@@ -55,7 +57,6 @@
     model = w_out_vm.shape[1]
     x = lax.rem(h, 2)
     y, k = i // 2, lax.rem(i, 2)
-    r_of_x = 2 * (1 - x)
     sib = (h, 2 * y + 1 - k)
     y_dev = (h, 2 * (1 - y) + k)
     x_dev = (h + 1 - 2 * x, i)
@@ -102,14 +103,15 @@
             own.at[1, dy, part(c), :], from_x.at[dy, part(c), :], a_s.at[dy, c], a_r.at[dy, c], x_dev
         )
 
-    def b_copy(half, c):
+    def b_copy(r, c):
         return remote(
-            own.at[2 * half, 1, part(c), :], from_y.at[half, part(c), :],
-            b_s.at[half, c], b_r.at[half, c], y_dev,
-        )
-
-    def z_copy(c):
-        return remote(own.at[2, 0, part(c), :], from_z.at[part(c), :], z_s.at[c], z_r.at[c], z_up)
+            own.at[r, 1, part(c), :], from_y.at[r, part(c), :], b_s.at[r, c], b_r.at[r, c], y_dev
+        )
+
+    def z_copy(dy, c):
+        return remote(
+            own.at[2, dy, part(c), :], from_z.at[dy, part(c), :], z_s.at[dy, c], z_r.at[dy, c], z_up
+        )
 
     loads = [
         pltpu.make_async_copy(tok_ref, x_ref.at[0, 0, pl.ds(0, tok), :], local_sem.at[0]),
@@ -199,8 +201,27 @@
         total = own[r, dy, part(c), :].astype(jnp.float32)
         total = total + sib_in[r, dy, part(c), :].astype(jnp.float32)
         for term in more:
-            total = total + term.astype(jnp.float32)
-        return total
+            total = total + term[part(c), :].astype(jnp.float32)
+        return total.astype(jnp.bfloat16)
+
+    def settle(r, dy, c, *more):
+        own[r, dy, part(c), :] = add_up(r, dy, c, *more)
+
+    def spread_near(c):
+        got((1, 0, 0), c)
+        if c in LATE:
+            x_copy((1, 1, 0), c, held(1, 0, c), y_dev).start()
+        x_copy((1, 0, 1), c, held(1, 0, c), sib).start()
+
+    def spread_far(c):
+        got((2, 1, 0), c)
+        if c in EARLY:
+
+            @pl.when(x == 0)
+            def _():
+                x_copy((1, 1, 0), c, held(2, 1, c), x_dev).start()
+
+        x_copy((2, 1, 1), c, held(2, 1, c), sib).start()
 
     for load in loads:
         load.wait()
@@ -212,71 +233,125 @@
         def _():
             x_copy((1, 0, 0), c, held(2, 0, c), x_dev).start()
 
-        x_copy((2, 1, 0), c, held(2, 0, c), y_dev).start()
+        if c in LATE:
+            x_copy((2, 1, 0), c, held(2, 0, c), y_dev).start()
         x_copy((2, 0, 1), c, held(2, 0, c), sib).start()
         got((0, 1, 0), c)
-
-        @pl.when(x == 1)
-        def _():
-            x_copy((1, 1, 0), c, held(0, 1, c), x_dev).start()
+        if c in EARLY:
+            x_copy((2, 1, 0), c, held(0, 1, c), z_down).start()
+
+            @pl.when(x == 1)
+            def _():
+                x_copy((1, 1, 0), c, held(0, 1, c), x_dev).start()
 
         x_copy((0, 1, 1), c, held(0, 1, c), sib).start()
-    compute(0, 1)
+        if c > 0:
+            spread_near(c - 1)
+    spread_near(CHUNKS - 1)
+    compute(1, 0)
+    spread_far(0)
     compute(2, 0)
-    for c in range(CHUNKS):
-        got((1, 0, 0), c)
-        x_copy((1, 0, 1), c, held(1, 0, c), sib).start()
-        got((2, 1, 0), c)
-
-        @pl.when(x == 0)
-        def _():
-            x_copy((1, 1, 0), c, held(2, 1, c), x_dev).start()
-
-        x_copy((2, 1, 1), c, held(2, 1, c), sib).start()
-    compute(1, 0)
+    q_copy(1, 0).wait_recv()
+    for c in EARLY:
+        settle(1, 0, c)
+        a_copy(0, c).start()
+    for c in range(1, CHUNKS):
+        spread_far(c)
+    q_copy(2, 0).wait_recv()
+
+    @pl.when(x == 1)
+    def _():
+        for c in EARLY:
+            settle(2, 0, c)
+            z_copy(0, c).start()
+
     compute(2, 1)
-    q_copy(1, 0).wait_recv()
-    for c in range(CHUNKS):
-        own[1, 0, part(c), :] = add_up(1, 0, c).astype(jnp.bfloat16)
-        a_copy(0, c).start()
-    q_copy(0, 1).wait_recv()
-    q_copy(2, 1).wait_recv()
-    r_plain = 2 - r_of_x
-    for c in range(CHUNKS):
-        own[r_plain, 1, part(c), :] = add_up(r_plain, 1, c).astype(jnp.bfloat16)
-        b_copy(r_plain // 2, c).start()
     for c in range(CHUNKS):
         got((1, 1, 0), c)
         x_copy((1, 1, 1), c, held(1, 1, c), sib).start()
+    q_copy(2, 1).wait_recv()
+    for c in LATE:
+        settle(2, 1, c)
+        b_copy(2, c).start()
+
+    @pl.when(x == 1)
+    def _():
+        for c in EARLY:
+            settle(2, 1, c)
+            z_copy(1, c).start()
+
     compute(1, 1)
     q_copy(1, 1).wait_recv()
+    for c in LATE:
+        settle(1, 1, c)
+        b_copy(1, c).start()
+    for c in EARLY:
+        settle(1, 1, c)
+        a_copy(1, c).start()
+
+    @pl.when(x == 0)
+    def _():
+        for c in EARLY:
+            a_copy(0, c).wait_recv()
+            settle(2, 0, c, from_x.at[0])
+            z_copy(0, c).start()
+
+    compute(0, 1)
+    for c in LATE:
+        b_copy(1, c).wait_recv()
+        settle(1, 0, c, from_y.at[1])
+        a_copy(0, c).start()
+    q_copy(0, 1).wait_recv()
+    for c in LATE:
+        settle(0, 1, c)
+        b_copy(0, c).start()
+
+    @pl.when(x == 0)
+    def _():
+        for c in EARLY:
+            a_copy(1, c).wait_recv()
+            settle(2, 1, c, from_x.at[1])
+            z_copy(1, c).start()
+
+    for c in LATE:
+        b_copy(2, c).wait_recv()
+
+        @pl.when(x == 0)
+        def _():
+            a_copy(0, c).wait_recv()
+            settle(2, 0, c, from_y.at[2], from_x.at[0])
+
+        @pl.when(x == 1)
+        def _():
+            settle(2, 0, c, from_y.at[2])
+
+        z_copy(0, c).start()
+    for c in EARLY:
+        z_copy(1, c).wait_recv()
+
+        @pl.when(x == 0)
+        def _():
+            settle(0, 1, c, from_z.at[1])
+
+        @pl.when(x == 1)
+        def _():
+            a_copy(1, c).wait_recv()
+            settle(0, 1, c, from_z.at[1], from_x.at[1])
+
+        b_copy(0, c).start()
+    q_copy(0, 0).wait_recv()
     for c in range(CHUNKS):
-        own[1, 1, part(c), :] = add_up(1, 1, c).astype(jnp.bfloat16)
-        a_copy(1, c).start()
-    q_copy(0, 0).wait_recv()
-    q_copy(2, 0).wait_recv()
-    for c in range(CHUNKS):
-        a_copy(0, c).wait_recv()
-        own[r_of_x, 0, part(c), :] = add_up(r_of_x, 0, c, from_x[0, part(c), :]).astype(jnp.bfloat16)
-        own[r_plain, 0, part(c), :] = add_up(r_plain, 0, c).astype(jnp.bfloat16)
-    for c in range(CHUNKS):
-        a_copy(1, c).wait_recv()
-        own[r_of_x, 1, part(c), :] = add_up(r_of_x, 1, c, from_x[1, part(c), :]).astype(jnp.bfloat16)
-        b_copy(r_of_x // 2, c).start()
-    for c in range(CHUNKS):
-        b_copy(1, c).wait_recv()
-        own[2, 0, part(c), :] = (
-            own[2, 0, part(c), :].astype(jnp.float32) + from_y[1, part(c), :].astype(jnp.float32)
-        ).astype(jnp.bfloat16)
-        z_copy(c).start()
-    for c in range(CHUNKS):
+        z_copy(0, c).wait_recv()
         b_copy(0, c).wait_recv()
-        z_copy(c).wait_recv()
-        out_ref[part(c), :] = (
-            own[0, 0, part(c), :].astype(jnp.float32)
-            + from_y[0, part(c), :].astype(jnp.float32)
-            + from_z[part(c), :].astype(jnp.float32)
-        ).astype(jnp.bfloat16)
+
+        @pl.when(x == 0)
+        def _():
+            out_ref[part(c), :] = add_up(0, 0, c, from_z.at[0], from_y.at[0])
+
+        @pl.when(x == 1)
+        def _():
+            a_copy(0, c).wait_recv()
+            out_ref[part(c), :] = add_up(0, 0, c, from_z.at[0], from_y.at[0], from_x.at[0])
 
     for slot in slots:
         aux_copy(*slot).wait_send()
@@ -286,10 +361,15 @@
         for dy in range(2):
             q_copy(r, dy).wait_send()
     for c in range(CHUNKS):
-        for half in range(2):
-            a_copy(half, c).wait_send()
-            b_copy(half, c).wait_send()
-        z_copy(c).wait_send()
+        a_copy(0, c).wait_send()
+        b_copy(0, c).wait_send()
+        z_copy(0, c).wait_send()
+        if c in EARLY:
+            a_copy(1, c).wait_send()
+            z_copy(1, c).wait_send()
+        else:
+            b_copy(1, c).wait_send()
+            b_copy(2, c).wait_send()
 
 
 def on_device_kernel(tokens, expert_ids, route_weights, w_in, w_out):
@@ -318,8 +398,8 @@
             pltpu.VMEM((3, 2, tok, model), bf16),
             pltpu.VMEM((3, 2, tok, model), bf16),
             pltpu.VMEM((2, tok, model), bf16),
+            pltpu.VMEM((3, tok, model), bf16),
             pltpu.VMEM((2, tok, model), bf16),
-            pltpu.VMEM((tok, model), bf16),
             dma((3,)),
             dma((12, CHUNKS)),
             dma((12, CHUNKS)),
@@ -329,10 +409,10 @@
             dma((6,)),
             dma((2, CHUNKS)),
             dma((2, CHUNKS)),
+            dma((3, CHUNKS)),
+            dma((3, CHUNKS)),
             dma((2, CHUNKS)),
             dma((2, CHUNKS)),
-            dma((CHUNKS,)),
-            dma((CHUNKS,)),
         ],
         compiler_params=pltpu.CompilerParams(
             collective_id=0, has_side_effects=True, vmem_limit_bytes=58 * 1024 * 1024

time: 144 us -> 118 us (0.82)
  Pallas kernels: 140 us -> 114 us
    pallas_call x1, Pallas kernels: 140 us -> 114 us  [on_device_kernel(): pl.pallas_call(moe_kernel, out_shape=jax.ShapeDtypeStruct((tok, model), b...]
where the time goes in v2:
time: 118 us; the launch traced here: 117 us
  Pallas kernels  114 us (97%)
  local copies, waits for them, and re-layouts  2.29 us (2%)
  other arithmetic  1.32 us (1%)
    pallas_call x1, Pallas kernels, on_device_kernel(): pl.pallas_call(moe_kernel, out_shape=jax.ShapeDtypeStruct((tok, model), b...  114 us

profile of v2, /device:TPU:3, one launch (start us, length us, event | category | flops | bytes accessed | tf_op | source)
XLA Modules:
  0.0 117.4 jit_solution(10572410470567081980)
XLA Ops:
  0.0 1.3 %select_reduce_fusion.aux_ref = f32[16,128]{1,0:T(8,128)} fusion(f32[8,128]{1,0:T(8,128)} %bitcast.2, s32[8,128]{1,0:T(8,128)} %bitcast.3), kind=kLoop, calls=%fused_computation | loop fusion | flops 47104 | bytes 16384 | tf_op jit(solution)/shard_map/reduce_sum | solution.py:380
  1.3 113.8 %shard_map.55 = bf16[128,4096]{1,0:T(8,128)(2,1)} custom-call(bf16[128,4096]{1,0:T(8,128)(2,1)} %tok_ref.1, f32[16,128]{1,0:T(8,128)} %select_reduce_fusion.aux_ref, bf16[1,4096,768]{2,1,0:T(8,128)(2,1)} %w_in_ref.1, bf16[1,384,4096]{2,1,0:T(8,128)(2,1)} %w_out_ref.1), custom_call_target="tpu_custom_call" | custom-call | tf_op jit(solution)/shard_map/pallas_call | solution.py:385
  115.1 2.3 %copy.7 = bf16[128,4096]{1,0:T(8,128)(2,1)} copy(bf16[128,4096]{1,0:T(8,128)(2,1)} %shard_map.55) | data formatting | bytes 2097152
